TPU v7x, 512 devices: a whole 4x8x8 slice. The times are simulated.
512 devices in a mesh: ctx: 128 (over z, y, core), head: 4 (over x).
Axes of the slice: x: 4, y: 8, z: 8, core: 2. Of those that a mesh axis runs over, the one named last changes fastest.
Arguments:
- queries: bfloat16 [49152, 4096], P('ctx', 'head'), may hold values from -6 to 6
- keys: bfloat16 [49152, 1024], P(('ctx', 'head')), may hold values from -6 to 6
- values: bfloat16 [49152, 1024], P(('ctx', 'head')), may hold values from -6 to 6
- doc_lengths: int32 [512], replicated, may hold values from 1 to 1536, 49152 in all
Outputs:
- attended: bfloat16 [49152, 4096], P('ctx', 'head')
All inputs are finite; a program needn't handle non-finite values.
Results may differ from a plain program's by a relative error of at most 0.0075.
Values may be sent and summed in bfloat16 or wider, within the bound.
No kernel may reach another device: no remote copies, remote signals or barrier semaphores. Data moves between devices by JAX's collectives and lax.ppermute only.
A program may use at most 128 MiB of HBM per device.

v0:
```python
import math

import jax
import jax.numpy as jnp
from jax import lax
from jax.sharding import PartitionSpec as P

HD = 128
REACH = 4


def shifted(value, axis, steps):
    count = lax.axis_size(axis)
    initial, last = (max(0, -steps), min(count, count - steps))
    return lax.ppermute(value, axis, [(source, source + steps) for source in range(initial, last)])


def doc_index(positions, doc_ends):
    return jnp.sum((doc_ends[None, :] <= positions[:, None]).astype(jnp.int32), axis=1)


def doc_single(position, doc_ends):
    return jnp.sum((doc_ends <= position).astype(jnp.int32))


def attend(q_block, kv_pair, q_positions, k_positions, doc_ends):
    q_docs = doc_index(q_positions, doc_ends)
    k_docs = doc_index(k_positions, doc_ends)
    allowed = (
        (q_docs[:, None] == k_docs[None, :])
        & (k_positions[None, :] <= q_positions[:, None])
        & (k_positions[None, :] >= 0)
    )
    score_scale = 1.0 / math.sqrt(kv_pair.shape[3])
    outputs, peak_list, totals = ([], [], [])
    for kv_group in range(kv_pair.shape[2]):
        scores = (
            jnp.einsum(
                "qjd,kd->jqk",
                q_block[:, kv_group],
                kv_pair[0, :, kv_group],
                preferred_element_type=jnp.float32,
            )
            * score_scale
        )
        masked = jnp.where(allowed[None], scores, -1e30)
        maxima = jnp.max(masked, axis=2)
        weights = jnp.where(allowed[None], jnp.exp(scores - maxima[:, :, None]), 0.0)
        outputs.append(
            jnp.einsum(
                "jqk,kd->qjd",
                weights.astype(jnp.bfloat16),
                kv_pair[1, :, kv_group],
                preferred_element_type=jnp.float32,
            )
        )
        peak_list.append(maxima.T)
        totals.append(jnp.sum(weights, axis=2).T)
    return (jnp.stack(outputs, axis=1), jnp.stack(peak_list, axis=1), jnp.stack(totals, axis=1))


def empty_partial(rows, groups, per_group, head_size):
    return (
        jnp.zeros((rows, groups, per_group, head_size), jnp.float32),
        jnp.full((rows, groups, per_group), -1e30, jnp.float32),
        jnp.zeros((rows, groups, per_group), jnp.float32),
    )


def combine(first, second):
    top = jnp.maximum(first[1], second[1])
    scale_first = jnp.exp(first[1] - top)
    scale_second = jnp.exp(second[1] - top)
    merged = first[0] * scale_first[..., None] + second[0] * scale_second[..., None]
    return (merged, top, first[2] * scale_first + second[2] * scale_second)


def local(queries, keys, values, doc_lengths):
    stacked = jnp.stack([keys, values])
    gathered = lax.all_to_all(stacked, "head", split_axis=2, concat_axis=1, tiled=True)
    rows = queries.shape[0]
    head_size = HD
    groups = gathered.shape[2] // head_size
    q_block = queries.reshape(rows, groups, -1, head_size)
    kv_pair = gathered.reshape(2, rows, groups, head_size)
    doc_ends = jnp.cumsum(doc_lengths)
    device = lax.axis_index("ctx")
    local_positions = device * rows + jnp.arange(rows, dtype=jnp.int32)
    blank = empty_partial(rows, groups, q_block.shape[2], head_size)
    state = attend(q_block, kv_pair, local_positions, local_positions, doc_ends)
    carried = kv_pair
    for step in range(1, REACH + 1):
        carried = shifted(kv_pair, "ctx", step)
        key_positions = local_positions - step * rows
        needed = (key_positions[rows - 1] >= 0) & (
            doc_single(key_positions[rows - 1], doc_ends)
            == doc_single(local_positions[0], doc_ends)
        )
        piece = lax.cond(
            needed,
            lambda: attend(q_block, carried, local_positions, key_positions, doc_ends),
            lambda: blank,
        )
        state = combine(state, piece)
    result = state[0] / state[2][..., None]
    return result.astype(jnp.bfloat16).reshape(rows, -1)


def solution(mesh):
    placed = (P("ctx", "head"), P(("ctx", "head"), None), P(("ctx", "head"), None), P())
    return jax.shard_map(
        local, mesh=mesh, in_specs=placed, out_specs=P("ctx", "head"), check_vma=False
    )
```

profile of v0, /device:TPU:351, one launch (start us, length us, event | category | flops | bytes accessed | tf_op | source)
XLA Modules:
  0.0 99.8 jit_solution(11367505353050353216)
XLA Ops:
  0.0 1.1 %pad_maximum_fusion.12 = bf16[2,96,1024]{2,1,0:T(8,128)(2,1)S(1)} fusion(bf16[1,96,1024]{2,1,0:T(8,128)(2,1)} %bitcast.437, bf16[1,96,1024]{2,1,0:T(8,128)(2,1)} %bitcast.438), kind=kLoop, calls=%fused_computation.212 | loop fusion | flops 196608 | bytes 786432 | tf_op jit(solution)/shard_map/stack | solution.py:79
  1.1 1.1 %copy.126 = bf16[2,96,1024]{1,0,2:T(2,128)(2,1)} copy(bf16[2,96,1024]{2,1,0:T(8,128)(2,1)S(1)} %pad_maximum_fusion.12) | data formatting | bytes 786432 | tf_op jit(solution)/shard_map/stack | solution.py:79
  2.2 4.2 %all-to-all-start = ((bf16[2,96,1024]{1,0,2:T(2,128)(2,1)}), bf16[2,96,1024]{1,0,2:T(2,128)(2,1)S(1)}, u32[]{:S(2)}, u32[]{:S(2)}) async-start(bf16[2,96,1024]{1,0,2:T(2,128)(2,1)} %copy.126), calls=%async_computation | async-start | bytes 1048576 | tf_op jit(solution)/shard_map/all_to_all | solution.py:80
  7.1 0.6 slice.127
  8.8 0.6 slice.128
  9.4 0.6 slice.129
  10.0 0.6 slice.130
  12.5 3.9 %convert_reduce_fusion.13 = (s32[]{:T(128)}, s32[]{:T(128)}, s32[]{:T(128)}, s32[]{:T(128)}, s32[]{:T(128)}, /*index=5*/s32[512]{0:T(512)S(1)}) fusion(s32[]{:T(128)} %bitcast.123, s32[4,128]{1,0:T(4,128)S(1)} %reduce-window.9, s32[4]{0:T(128)S(1)} %slice_reduce_fusion, s32[]{:T(128)} %bitcast.124, s32[]{:T(128)} %bitcast.125, s32[]{:T(128)} %bitcast.126, ...), kind=kLoop, calls=%fused_computation.241 | loop fusion | flops 8187 | bytes 4152 | tf_op jit(solution)/shard_map/reduce_sum | solution.py:23
  22.5 4.5 %collective-permute-start.3 = (bf16[2,384,2,128]{3,2,1,0:T(2,128)(2,1)S(1)}, bf16[2,384,2,128]{3,2,1,0:T(2,128)(2,1)S(1)}, u32[]{:S(2)}, u32[]{:S(2)}) collective-permute-start(bf16[2,384,2,128]{3,2,1,0:T(2,128)(2,1)S(1)} %reshape.434), channel_id=1, source_target_pairs={{0,16},{4,20},{8,24},{12,28},{16,32},{20,36},{24,40},{28,44},{32,4... | collective-permute-start | bytes 1179656 | tf_op jit(solution)/shard_map/ppermute | solution.py:15
  27.0 3.8 %collective-permute-start.2 = (bf16[2,384,2,128]{3,2,1,0:T(2,128)(2,1)S(1)}, bf16[2,384,2,128]{3,2,1,0:T(2,128)(2,1)S(1)}, u32[]{:S(2)}, u32[]{:S(2)}) collective-permute-start(bf16[2,384,2,128]{3,2,1,0:T(2,128)(2,1)S(1)} %reshape.434), channel_id=1, source_target_pairs={{0,12},{4,16},{8,20},{12,24},{16,28},{20,32},{24,36},{28,40},{32,4... | collective-permute-start | bytes 1179656 | tf_op jit(solution)/shard_map/ppermute | solution.py:15
  30.9 2.3 %collective-permute-start.1 = (bf16[2,384,2,128]{3,2,1,0:T(2,128)(2,1)S(1)}, bf16[2,384,2,128]{3,2,1,0:T(2,128)(2,1)}, u32[]{:S(2)}, u32[]{:S(2)}) collective-permute-start(bf16[2,384,2,128]{3,2,1,0:T(2,128)(2,1)S(1)} %reshape.434), channel_id=1, source_target_pairs={{0,8},{4,12},{8,16},{12,20},{16,24},{20,28},{24,32},{28,36},{32,40... | collective-permute-start | bytes 1179656 | tf_op jit(solution)/shard_map/ppermute | solution.py:15
  33.2 2.1 %collective-permute-start = (bf16[2,384,2,128]{3,2,1,0:T(2,128)(2,1)S(1)}, bf16[2,384,2,128]{3,2,1,0:T(2,128)(2,1)}, u32[]{:S(2)}, u32[]{:S(2)}) collective-permute-start(bf16[2,384,2,128]{3,2,1,0:T(2,128)(2,1)S(1)} %reshape.434), channel_id=1, source_target_pairs={{0,4},{4,8},{8,12},{12,16},{16,20},{20,24},{24,28},{28,32},{32,36}... | collective-permute-start | bytes 1179656 | tf_op jit(solution)/shard_map/ppermute | solution.py:15
  36.7 1.7 %fusion.110 = (f32[4,384]{1,0:T(4,128)}, f32[4,384]{1,0:T(4,128)S(1)}, f32[384,384,4]{1,0,2:T(8,128)S(1)}) fusion(f32[384,384,4]{1,0,2:T(8,128)S(1)} %get-tuple-element.231, f32[4,384]{1,0:T(4,128)S(1)} %get-tuple-element.230, pred[384,384]{0,1:T(8,128)(4,1)S(1)} %and_and_fusion.4, bf16[384,2,4,128]{0,3,2,1:T(8,128)(2,1)S(1)} %bitcast.429, ...), kind=kOutput, calls=%fused_computation.182 | convolution fusion | flops 155120640 | bytes 5474304 | tf_op jit(solution)/shard_map/qjd,kd->jqk/dot_general | solution.py:38
  38.4 1.6 %convolution_bitcast_fusion.9 = f32[384,1,4,128]{0,3,2,1:T(8,128)} fusion(f32[384,384,4]{1,0,2:T(8,128)S(1)} %get-tuple-element.231, f32[4,384]{1,0:T(4,128)S(1)} %get-tuple-element.230, pred[384,384]{0,1:T(8,128)(4,1)S(1)} %and_and_fusion.4, bf16[1,384,1,128]{1,3,2,0:T(8,128)(2,1)S(1)} %copy.168), kind=kOutput, calls=%fused_computation.197 | convolution fusion | flops 153354240 | bytes 3397632 | tf_op jit(solution)/shard_map/jqk,kd->qjd/dot_general | solution.py:50
  39.9 1.5 %convolution_bitcast_fusion.8 = f32[384,1,4,128]{0,3,2,1:T(8,128)} fusion(f32[384,384,4]{1,0,2:T(8,128)S(1)} %get-tuple-element.232, f32[4,384]{1,0:T(4,128)S(1)} %get-tuple-element.190, pred[384,384]{0,1:T(8,128)(4,1)S(1)} %and_and_fusion.4, bf16[1,384,1,128]{1,3,2,0:T(8,128)(2,1)S(1)} %copy.171), kind=kOutput, calls=%fused_computation.196 | convolution fusion | flops 153354240 | bytes 3397632 | tf_op jit(solution)/shard_map/jqk,kd->qjd/dot_general | solution.py:50
  41.5 1.1 %fusion.112 = f32[4,384]{1,0:T(4,128)} fusion(f32[384,384,4]{1,0,2:T(8,128)S(1)} %get-tuple-element.232, f32[4,384]{1,0:T(4,128)S(1)} %get-tuple-element.190, pred[384,384]{0,1:T(8,128)(4,1)S(1)} %and_and_fusion.4), kind=kLoop, calls=%fused_computation.184 | loop fusion | flops 2357760 | bytes 2519040 | tf_op jit(solution)/shard_map/reduce_sum | solution.py:58
  42.6 4.6 %collective-permute-done.3 = bf16[2,384,2,128]{3,2,1,0:T(2,128)(2,1)S(1)} collective-permute-done((bf16[2,384,2,128]{3,2,1,0:T(2,128)(2,1)S(1)}, bf16[2,384,2,128]{3,2,1,0:T(2,128)(2,1)S(1)}, u32[]{:S(2)}, u32[]{:S(2)}) %collective-permute-start.3) | collective-permute-done | bytes 393248 | tf_op jit(solution)/shard_map/ppermute | solution.py:15
  47.3 12.8 %collective-permute-done.2 = bf16[2,384,2,128]{3,2,1,0:T(2,128)(2,1)S(1)} collective-permute-done((bf16[2,384,2,128]{3,2,1,0:T(2,128)(2,1)S(1)}, bf16[2,384,2,128]{3,2,1,0:T(2,128)(2,1)S(1)}, u32[]{:S(2)}, u32[]{:S(2)}) %collective-permute-start.2) | collective-permute-done | bytes 393248 | tf_op jit(solution)/shard_map/ppermute | solution.py:15
  60.1 13.6 %conditional.6 = (f32[384,2,4]{0,2,1:T(4,128)S(1)}, f32[384,2,4]{0,2,1:T(4,128)S(1)}, f32[384,2,4,128]{0,3,2,1:T(8,128)}) conditional(s32[]{:T(128)} %convert_element_type.105, () %tuple.41, (s32[512]{0:T(512)S(1)}, s32[384]{0:T(512)S(1)}, s32[384]{0:T(512)}, bf16[2,384,2,128]{3,2,1,0:T(2,128)(2,1)S(1)}, ...), branch_computations={%region_25.26_spmd, %region_26.33_spmd} | conditional | flops 619118208 | bytes 28721488 | solution.py:99
  60.1 1.0 convert_reduce_fusion.4
  61.0 0.7 broadcast_compare_fusion.2
  61.7 1.5 %and_and_fusion.2 = pred[384,384]{0,1:T(8,128)(4,1)} fusion(s32[384]{0:T(512)S(1)} %get-tuple-element.56, s32[384]{0:T(512)S(1)} %get-tuple-element.184, s32[384]{0:T(512)} %get-tuple-element.57, s32[384]{0:T(512)S(1)} %get-tuple-element.183, pred[384]{0:T(512)(128)(4,1)S(1)} %broadcast_compare_fusion.2), kind=kLoop, calls=%fused_computation.113 | loop fusion | flops 589824 | bytes 153984 | tf_op jit(solution)/shard_map/cond/branch_1_fun/and | solution.py:30
  63.7 1.1 %copy.143 = bf16[2,384,2,128]{3,1,2,0:T(8,128)(2,1)S(1)} copy(bf16[2,384,2,128]{3,2,1,0:T(2,128)(2,1)} %copy-done.3) | data formatting | bytes 786432 | tf_op jit(solution)/shard_map
  64.7 1.5 %fusion.55 = (f32[4,384]{1,0:T(4,128)S(1)}, f32[384,384,4]{1,0,2:T(8,128)S(1)}) fusion(pred[384,384]{0,1:T(8,128)(4,1)} %and_and_fusion.2, bf16[384,2,4,128]{3,0,2,1:T(8,128)(2,1)S(1)} %copy.144, bf16[2,384,2,128]{3,1,2,0:T(8,128)(2,1)S(1)} %copy.143), kind=kOutput, calls=%fused_computation.93 | convolution fusion | flops 152762880 | bytes 3004416 | tf_op jit(solution)/shard_map/cond/branch_1_fun/qjd,kd->jqk/dot_general | solution.py:38
  66.2 1.1 %fusion.58 = (f32[4,384]{1,0:T(4,128)S(1)}, f32[4,384]{1,0:T(4,128)S(1)}, f32[384,384,4]{1,0,2:T(8,128)S(1)}) fusion(f32[384,384,4]{1,0,2:T(8,128)S(1)} %get-tuple-element.216, f32[4,384]{1,0:T(4,128)S(1)} %get-tuple-element.215, pred[384,384]{0,1:T(8,128)(4,1)S(1)} %copy-done, bf16[384,2,4,128]{3,0,2,1:T(8,128)(2,1)S(1)} %copy.144, ...), kind=kOutput, calls=%fused_computation.96 | convolution fusion | flops 155120640 | bytes 5376000 | tf_op jit(solution)/shard_map/cond/branch_1_fun/qjd,kd->jqk/dot_general | solution.py:38
  67.9 0.7 convolution_bitcast_fusion.4
  68.6 0.7 convolution_bitcast_fusion.5
  69.3 1.3 %pad_maximum_fusion.6 = f32[384,2,4,128]{3,0,2,1:T(8,128)} fusion(f32[384,1,4,128]{3,0,2,1:T(8,128)S(1)} %convolution_bitcast_fusion.4, f32[384,1,4,128]{3,0,2,1:T(8,128)S(1)} %convolution_bitcast_fusion.5), kind=kLoop, calls=%fused_computation.100 | loop fusion | flops 393216 | bytes 3145728 | tf_op jit(solution)/shard_map/cond/branch_1_fun/stack | solution.py:59
  70.6 3.0 %copy.165 = f32[384,2,4,128]{0,3,2,1:T(8,128)} copy(f32[384,2,4,128]{3,0,2,1:T(8,128)} %pad_maximum_fusion.6) | data formatting | bytes 3145728 | tf_op jit(solution)/shard_map/cond | solution.py:99
  73.7 0.6 copy-done.11
  74.2 11.6 %conditional.5 = (f32[384,2,4]{0,2,1:T(4,128)S(1)}, f32[384,2,4]{0,2,1:T(4,128)S(1)}, f32[384,2,4,128]{0,3,2,1:T(8,128)}) conditional(s32[]{:T(128)} %convert_element_type.103, () %tuple.39, (s32[512]{0:T(512)S(1)}, s32[384]{0:T(512)S(1)}, s32[384]{0:T(512)S(1)}, bf16[2,384,2,128]{3,2,1,0:T(2,128)(2,1)}, ...), branch_computations={%region_16.17_spmd, %region_17.24_spmd} | conditional | flops 619118208 | bytes 27148596 | solution.py:99
  74.6 0.9 and_and_fusion.1
  75.9 1.1 %copy.140 = bf16[2,384,2,128]{3,1,2,0:T(8,128)(2,1)S(1)} copy(bf16[2,384,2,128]{3,2,1,0:T(2,128)(2,1)} %get-tuple-element.157) | data formatting | bytes 786432 | tf_op jit(solution)/shard_map
  76.9 1.5 %fusion.29 = (f32[4,384]{1,0:T(4,128)S(1)}, f32[384,384,4]{1,0,2:T(8,128)S(1)}) fusion(pred[384,384]{0,1:T(8,128)(4,1)} %and_and_fusion.1, bf16[384,2,4,128]{3,0,2,1:T(8,128)(2,1)S(1)} %copy.141, bf16[2,384,2,128]{3,1,2,0:T(8,128)(2,1)S(1)} %copy.140), kind=kOutput, calls=%fused_computation.50 | convolution fusion | flops 152762880 | bytes 3004416 | tf_op jit(solution)/shard_map/cond/branch_1_fun/qjd,kd->jqk/dot_general | solution.py:38
  78.4 1.1 %fusion.32 = (f32[4,384]{1,0:T(4,128)S(1)}, f32[4,384]{1,0:T(4,128)S(1)}, f32[384,384,4]{1,0,2:T(8,128)S(1)}) fusion(f32[384,384,4]{1,0,2:T(8,128)S(1)} %get-tuple-element.211, f32[4,384]{1,0:T(4,128)S(1)} %get-tuple-element.210, pred[384,384]{0,1:T(8,128)(4,1)S(1)} %copy-done.1, bf16[384,2,4,128]{3,0,2,1:T(8,128)(2,1)S(1)} %copy.141, ...), kind=kOutput, calls=%fused_computation.53 | convolution fusion | flops 155120640 | bytes 5376000 | tf_op jit(solution)/shard_map/cond/branch_1_fun/qjd,kd->jqk/dot_general | solution.py:38
  80.1 0.7 convolution_bitcast_fusion.2
  80.8 0.7 convolution_bitcast_fusion.3
  81.5 1.3 %pad_maximum_fusion.3 = f32[384,2,4,128]{3,0,2,1:T(8,128)} fusion(f32[384,1,4,128]{3,0,2,1:T(8,128)S(1)} %convolution_bitcast_fusion.2, f32[384,1,4,128]{3,0,2,1:T(8,128)S(1)} %convolution_bitcast_fusion.3), kind=kLoop, calls=%fused_computation.57 | loop fusion | flops 393216 | bytes 3145728 | tf_op jit(solution)/shard_map/cond/branch_1_fun/stack | solution.py:59
  82.8 3.0 %copy.163 = f32[384,2,4,128]{0,3,2,1:T(8,128)} copy(f32[384,2,4,128]{3,0,2,1:T(8,128)} %pad_maximum_fusion.3) | data formatting | bytes 3145728 | tf_op jit(solution)/shard_map/cond | solution.py:99
  86.5 7.4 %conditional.4 = (f32[384,2,4]{0,2,1:T(4,128)S(1)}, f32[384,2,4]{0,2,1:T(4,128)S(1)}, f32[384,2,4,128]{0,3,2,1:T(8,128)}) conditional(s32[]{:T(128)} %convert_element_type.101, () %tuple.37, (s32[512]{0:T(512)S(1)}, s32[384]{0:T(512)S(1)}, s32[384]{0:T(512)S(1)}, bf16[2,384,2,128]{3,2,1,0:T(2,128)(2,1)}, ...), branch_computations={%region_7.8_spmd, %region_8.15_spmd} | conditional | flops 619118208 | bytes 26558744 | solution.py:99
  87.4 1.1 %copy.137 = bf16[2,384,2,128]{3,1,2,0:T(8,128)(2,1)S(1)} copy(bf16[2,384,2,128]{3,2,1,0:T(2,128)(2,1)} %get-tuple-element.152) | data formatting | bytes 786432 | tf_op jit(solution)/shard_map
  89.0 1.1 %fusion.6 = (f32[4,384]{1,0:T(4,128)S(1)}, f32[4,384]{1,0:T(4,128)S(1)}, f32[384,384,4]{1,0,2:T(8,128)S(1)}) fusion(f32[384,384,4]{1,0,2:T(8,128)S(1)} %get-tuple-element.206, f32[4,384]{1,0:T(4,128)S(1)} %get-tuple-element.205, pred[384,384]{0,1:T(8,128)(4,1)S(1)} %and_and_fusion, bf16[384,2,4,128]{3,0,2,1:T(8,128)(2,1)S(1)} %copy.138, ...), kind=kOutput, calls=%fused_computation.10 | convolution fusion | flops 155120640 | bytes 5376000 | tf_op jit(solution)/shard_map/cond/branch_1_fun/qjd,kd->jqk/dot_general | solution.py:38
  90.7 0.7 convolution_bitcast_fusion
  91.4 0.7 convolution_bitcast_fusion.1
  92.2 1.6 %copy.161 = f32[384,2,4,128]{0,3,2,1:T(8,128)} copy(f32[384,2,4,128]{3,0,2,1:T(8,128)S(1)} %pad_maximum_fusion) | data formatting | bytes 3145728 | tf_op jit(solution)/shard_map/cond | solution.py:99
  93.9 0.8 fusion.145
  94.7 4.0 %fusion.122 = bf16[384,2,4,128]{0,3,2,1:T(8,128)(2,1)S(1)} fusion(f32[384,2,4,128]{0,3,2,1:T(8,128)S(1)} %get-tuple-element.172, f32[384,2,4,128]{0,3,2,1:T(8,128)} %get-tuple-element.171, f32[384,2,4,128]{0,3,2,1:T(8,128)} %get-tuple-element.170, f32[384,2,4,128]{0,3,2,1:T(8,128)} %get-tuple-element.169, f32[384,1,4,128]{0,3,2,1:T(8,128)} %convolution_bitcast_fusion.8, ...), kind=kLoop, calls=%fused_computation.195 | loop fusion | flops 5898240 | bytes 8761344 | tf_op jit(solution)/shard_map/convert_element_type | solution.py:106
  98.7 1.2 %copy.149 = bf16[384,1024]{1,0:T(8,128)(2,1)} copy(bf16[384,1024]{0,1:T(8,128)(2,1)S(1)} %bitcast.434) | data formatting | bytes 1572864 | tf_op jit(solution)/shard_map/reshape | solution.py:106
  (86 shorter events, 8.9 us)
Async XLA Ops:
  0.0 8.3 %copy-start.21 = (s32[512]{0:T(512)S(1)}, s32[512]{0:T(512)}, u32[]{:S(2)}) copy-start(s32[512]{0:T(512)} %param.15) | copy-start | bytes 6148
  0.0 17.5 %copy-start.2 = (bf16[384,1024]{1,0:T(8,128)(2,1)S(1)}, bf16[384,1024]{1,0:T(8,128)(2,1)}, u32[]{:S(2)}) copy-start(bf16[384,1024]{1,0:T(8,128)(2,1)} %param.12) | copy-start | bytes 2359300
  2.2 19.7 %all-to-all-start = ((bf16[2,96,1024]{1,0,2:T(2,128)(2,1)}), bf16[2,96,1024]{1,0,2:T(2,128)(2,1)S(1)}, u32[]{:S(2)}, u32[]{:S(2)}) async-start(bf16[2,96,1024]{1,0,2:T(2,128)(2,1)} %copy.126), calls=%async_computation | async-start | bytes 1048576 | tf_op jit(solution)/shard_map/all_to_all | solution.py:80
  6.5 6.0 %copy-start.14 = (s32[384]{0:T(512)}, s32[384]{0:T(512)S(1)}, u32[]{:S(2)}) copy-start(s32[384]{0:T(512)S(1)} %fusion.148) | copy-start | bytes 4612
  22.5 24.6 %collective-permute-start.3 = (bf16[2,384,2,128]{3,2,1,0:T(2,128)(2,1)S(1)}, bf16[2,384,2,128]{3,2,1,0:T(2,128)(2,1)S(1)}, u32[]{:S(2)}, u32[]{:S(2)}) collective-permute-start(bf16[2,384,2,128]{3,2,1,0:T(2,128)(2,1)S(1)} %reshape.434), channel_id=1, source_target_pairs={{0,16},{4,20},{8,24},{12,28},{16,32},{20,36},{24,40},{28,44},{32,4... | collective-permute-start | bytes 1179656 | tf_op jit(solution)/shard_map/ppermute | solution.py:15
  27.0 33.0 %collective-permute-start.2 = (bf16[2,384,2,128]{3,2,1,0:T(2,128)(2,1)S(1)}, bf16[2,384,2,128]{3,2,1,0:T(2,128)(2,1)S(1)}, u32[]{:S(2)}, u32[]{:S(2)}) collective-permute-start(bf16[2,384,2,128]{3,2,1,0:T(2,128)(2,1)S(1)} %reshape.434), channel_id=1, source_target_pairs={{0,12},{4,16},{8,20},{12,24},{16,28},{20,32},{24,36},{28,40},{32,4... | collective-permute-start | bytes 1179656 | tf_op jit(solution)/shard_map/ppermute | solution.py:15
  30.9 42.8 %collective-permute-start.1 = (bf16[2,384,2,128]{3,2,1,0:T(2,128)(2,1)S(1)}, bf16[2,384,2,128]{3,2,1,0:T(2,128)(2,1)}, u32[]{:S(2)}, u32[]{:S(2)}) collective-permute-start(bf16[2,384,2,128]{3,2,1,0:T(2,128)(2,1)S(1)} %reshape.434), channel_id=1, source_target_pairs={{0,8},{4,12},{8,16},{12,20},{16,24},{20,28},{24,32},{28,36},{32,40... | collective-permute-start | bytes 1179656 | tf_op jit(solution)/shard_map/ppermute | solution.py:15
  33.2 52.7 %collective-permute-start = (bf16[2,384,2,128]{3,2,1,0:T(2,128)(2,1)S(1)}, bf16[2,384,2,128]{3,2,1,0:T(2,128)(2,1)}, u32[]{:S(2)}, u32[]{:S(2)}) collective-permute-start(bf16[2,384,2,128]{3,2,1,0:T(2,128)(2,1)S(1)} %reshape.434), channel_id=1, source_target_pairs={{0,4},{4,8},{8,12},{12,16},{16,20},{20,24},{24,28},{28,32},{32,36}... | collective-permute-start | bytes 1179656 | tf_op jit(solution)/shard_map/ppermute | solution.py:15
  36.7 1.7 %copy-start.15 = (f32[4,384]{1,0:T(4,128)}, f32[4,384]{1,0:T(4,128)S(1)}, u32[]{:S(2)}) copy-start(f32[4,384]{1,0:T(4,128)S(1)} %get-tuple-element.230) | copy-start | bytes 18436
  38.4 3.1 %copy-start.17 = (f32[4,384]{1,0:T(4,128)}, f32[4,384]{1,0:T(4,128)S(1)}, u32[]{:S(2)}) copy-start(f32[4,384]{1,0:T(4,128)S(1)} %get-tuple-element.190) | copy-start | bytes 18436
  47.3 12.8 %copy-start.9 = (f32[384,2,4]{0,2,1:T(4,128)}, f32[384,2,4]{0,2,1:T(4,128)S(1)}, u32[]{:S(2)}) copy-start(f32[384,2,4]{0,2,1:T(4,128)S(1)} %get-tuple-element.88) | copy-start | bytes 36868
  47.3 12.8 %copy-start.4 = (f32[384,2,4]{0,2,1:T(4,128)}, f32[384,2,4]{0,2,1:T(4,128)S(1)}, u32[]{:S(2)}) copy-start(f32[384,2,4]{0,2,1:T(4,128)S(1)} %get-tuple-element.83) | copy-start | bytes 36868
  60.1 3.2 %copy-start.3 = (bf16[2,384,2,128]{3,2,1,0:T(2,128)(2,1)}, bf16[2,384,2,128]{3,2,1,0:T(2,128)(2,1)S(1)}, u32[]{:S(2)}) copy-start(bf16[2,384,2,128]{3,2,1,0:T(2,128)(2,1)S(1)} %get-tuple-element.162) | copy-start | bytes 1179652 | tf_op jit(solution)/shard_map/cond
  63.6 2.6 %copy-start = (pred[384,384]{0,1:T(8,128)(4,1)S(1)}, pred[384,384]{0,1:T(8,128)(4,1)}, u32[]{:S(2)}) copy-start(pred[384,384]{0,1:T(8,128)(4,1)} %and_and_fusion.2) | copy-start | bytes 442372 | tf_op jit(solution)/shard_map/cond
  73.6 0.6 copy-start.11
  73.6 0.6 copy-start.6
  75.8 2.6 %copy-start.1 = (pred[384,384]{0,1:T(8,128)(4,1)S(1)}, pred[384,384]{0,1:T(8,128)(4,1)}, u32[]{:S(2)}) copy-start(pred[384,384]{0,1:T(8,128)(4,1)} %and_and_fusion.1) | copy-start | bytes 442372 | tf_op jit(solution)/shard_map/cond
  85.9 0.6 copy-start.8
  85.9 0.6 copy-start.13
  85.9 8.0 %copy-start.5 = (f32[384,2,4]{0,2,1:T(4,128)S(1)}, f32[384,2,4]{0,2,1:T(4,128)}, u32[]{:S(2)}) copy-start(f32[384,2,4]{0,2,1:T(4,128)} %copy-done.4) | copy-start | bytes 36868
  85.9 8.0 %copy-start.7 = (f32[384,2,4]{0,2,1:T(4,128)S(1)}, f32[384,2,4]{0,2,1:T(4,128)}, u32[]{:S(2)}) copy-start(f32[384,2,4]{0,2,1:T(4,128)} %copy-done.6) | copy-start | bytes 36868
  85.9 8.0 %copy-start.10 = (f32[384,2,4]{0,2,1:T(4,128)S(1)}, f32[384,2,4]{0,2,1:T(4,128)}, u32[]{:S(2)}) copy-start(f32[384,2,4]{0,2,1:T(4,128)} %copy-done.9) | copy-start | bytes 36868
  85.9 8.0 %copy-start.12 = (f32[384,2,4]{0,2,1:T(4,128)S(1)}, f32[384,2,4]{0,2,1:T(4,128)}, u32[]{:S(2)}) copy-start(f32[384,2,4]{0,2,1:T(4,128)} %copy-done.11) | copy-start | bytes 36868
  85.9 8.0 %copy-start.16 = (f32[4,384]{1,0:T(4,128)S(1)}, f32[4,384]{1,0:T(4,128)}, u32[]{:S(2)}) copy-start(f32[4,384]{1,0:T(4,128)} %copy-done.15) | copy-start | bytes 18436
  85.9 8.0 %copy-start.18 = (f32[4,384]{1,0:T(4,128)S(1)}, f32[4,384]{1,0:T(4,128)}, u32[]{:S(2)}) copy-start(f32[4,384]{1,0:T(4,128)} %copy-done.17) | copy-start | bytes 18436
  85.9 8.0 %copy-start.19 = (f32[4,384]{1,0:T(4,128)S(1)}, f32[4,384]{1,0:T(4,128)}, u32[]{:S(2)}) copy-start(f32[4,384]{1,0:T(4,128)} %fusion.112) | copy-start | bytes 18436
  85.9 8.0 %copy-start.20 = (f32[4,384]{1,0:T(4,128)S(1)}, f32[4,384]{1,0:T(4,128)}, u32[]{:S(2)}) copy-start(f32[4,384]{1,0:T(4,128)} %get-tuple-element.189) | copy-start | bytes 18436
where the time goes:
time: 101 us; the launch traced here: 99.8 us
  other arithmetic  20.9 us (21%)
  local copies, waits for them, and re-layouts  20.4 us (20%)
  waiting for transfers between devices  17.3 us (17%)
  starting transfers between devices  17 us (17%)
  matrix products  16.4 us (16%)
  between operations  7.57 us (7%)
    ppermute x4, waiting for transfers between devices, shifted(): lax.ppermute(value, axis, [(source, source + steps) for source in range(i...  17.3 us
    ppermute x4, starting transfers between devices, shifted(): lax.ppermute(value, axis, [(source, source + steps) for source in range(i...  12.7 us
    dot_general x8, matrix products, attend(): jnp.einsum('qjd,kd->jqk', q_block[:, kv_group], kv_pair[0, :, kv_group],...  8.98 us
    cond x3, local copies, waits for them, and re-layouts, local(): lax.cond(needed, lambda: attend(q_block, carried, local_positions, key_po...  7.67 us
    dot_general x8, matrix products, attend(): jnp.einsum('jqk,kd->qjd', weights.astype(jnp.bfloat16), kv_pair[1, :, kv_...  7.46 us
    another operation x7, local copies, waits for them, and re-layouts  4.47 us
    all_to_all x1, starting transfers between devices, local(): lax.all_to_all(stacked, 'head', split_axis=2, concat_axis=1, tiled=True)  4.21 us
    convert_element_type x1, other arithmetic, local(): return result.astype(jnp.bfloat16).reshape(rows, -1)  3.96 us
  transfers between devices with their start and end apart: 5, of which 2 were waited for; matrix products, arithmetic and copies ran while one was open for 41% of the time, Pallas kernels for 0%

commit v1 on v0

v1 whole, which is shorter than its diff:
```python
import functools
import math

import jax
import jax.numpy as jnp
from jax import lax
from jax.experimental import pallas as pl
from jax.experimental.pallas import tpu as pltpu
from jax.sharding import PartitionSpec as P

HD = 128
GROUPS = 2
PER = 4
HEADS = GROUPS * PER
CORES = 2
MASKED = -1e30
TILE = 128
SCALE = math.log2(math.e) / math.sqrt(HD)
VMEM = 40 * 1024 * 1024


def shifted(value, steps):
    count = lax.axis_size("ctx")
    return lax.ppermute(value, "ctx", [(at, at + steps) for at in range(count - steps)])


def both_cores(value):
    count = lax.axis_size("ctx")
    pairs = [[at + core for core in range(CORES)] for at in range(0, count, CORES)]
    return lax.all_gather(value, "ctx", axis=0, tiled=True, axis_index_groups=pairs)


def pack_kernel(k_ref, v_ref, out_ref):
    for kind, ref in enumerate((k_ref, v_ref)):
        for column in range(out_ref.shape[0] * GROUPS):
            part = ref[:, column * HD : (column + 1) * HD]
            out_ref[column // GROUPS, kind, column % GROUPS] = part


def pack(keys, values, targets):
    rows = keys.shape[0]
    return pl.pallas_call(
        pack_kernel,
        out_shape=jax.ShapeDtypeStruct((targets, 2, GROUPS, rows, HD), keys.dtype),
        name="pack",
    )(keys, values)


def query_tile(q_ref, group, row):
    heads = [
        q_ref[pl.ds(row, TILE), (group * PER + j) * HD : (group * PER + j + 1) * HD]
        for j in range(PER)
    ]
    return jnp.concatenate(heads, axis=0)


def chunk(kv_ref, kind, group, first, count):
    blocks = kv_ref[first : first + count, kind, group]
    return blocks.reshape(count * blocks.shape[1], HD)


def with_ones(values):
    return jnp.concatenate([values, jnp.ones_like(values)], axis=1)


def score(queries, keys, bias):
    raw = lax.dot_general(
        queries, keys, (((1,), (1,)), ((), ())), preferred_element_type=jnp.float32
    )
    return raw.reshape(PER, TILE, -1) + bias[None]


def weigh(raw, top, values):
    weights = jnp.exp2((raw - top) * SCALE).astype(jnp.bfloat16)
    summed = jnp.dot(
        weights.reshape(PER * TILE, -1), with_ones(values), preferred_element_type=jnp.float32
    )
    return summed.reshape(PER, TILE, 2 * HD)


def doc_starts(lengths_ref, starts_ref, first):
    lengths = lengths_ref[...]
    docs = lengths.shape[1]
    earlier = lax.broadcasted_iota(jnp.int32, (docs, docs), 0) < lax.broadcasted_iota(
        jnp.int32, (docs, docs), 1
    )
    earlier = earlier.astype(jnp.bfloat16)

    def before(part):
        part = jnp.broadcast_to(part.astype(jnp.float32), (16, docs)).astype(jnp.bfloat16)
        return jnp.dot(part, earlier, preferred_element_type=jnp.float32)[0:1]

    begins = before(lengths >> 4) * 16.0 + before(lengths & 15)
    rows = starts_ref.shape[0]
    for row in range(0, rows, TILE):
        at = lax.broadcasted_iota(jnp.int32, (TILE, docs), 0) + (first + row)
        at = at.astype(jnp.float32)
        found = jnp.max(jnp.where(begins <= at, begins, 0.0), axis=1, keepdims=True)
        starts_ref[row : row + TILE] = jnp.broadcast_to(found, (TILE, HD))


def own_kernel(lengths_ref, q_ref, kv_ref, starts_ref, acc_ref, sum_ref, top_ref):
    rows = q_ref.shape[0]
    part = kv_ref.shape[3]
    blocks = rows // part
    device = lax.axis_index("ctx")
    core = lax.rem(device, CORES)
    doc_starts(lengths_ref, starts_ref, device * rows)

    def run(earlier):
        for tile in range(rows // TILE):
            row = tile * TILE
            used = -(-(row + TILE) // part) + earlier * blocks
            keys = used * part
            at_key = lax.broadcasted_iota(jnp.int32, (TILE, keys), 1) - earlier * rows
            at_query = lax.broadcasted_iota(jnp.int32, (TILE, keys), 0) + row
            since = starts_ref[row : row + TILE, 0:1] - (device * rows).astype(jnp.float32)
            allowed = (at_key <= at_query) & (at_key.astype(jnp.float32) >= since)
            bias = jnp.where(allowed, 0.0, MASKED)
            for group in range(GROUPS):
                queries = query_tile(q_ref, group, row)
                raw = score(queries, chunk(kv_ref, 0, group, 0, used), bias)
                top = jnp.max(raw, axis=2, keepdims=True)
                summed = weigh(raw, top, chunk(kv_ref, 1, group, 0, used))
                heads = pl.ds(group * PER, PER)
                acc_ref[heads, row : row + TILE] = summed[:, :, :HD]
                sum_ref[heads, row : row + TILE] = summed[:, :, HD:]
                top_ref[heads, row : row + TILE] = jnp.broadcast_to(top, (PER, TILE, HD))

    for which in range(CORES):
        pl.when(core == which)(functools.partial(run, which))


def update(q_ref, kv_ref, starts_ref, state, tile, base, first, count):
    acc_ref, sum_ref, top_ref = state
    part = kv_ref.shape[3]
    row = tile * TILE
    at_key = lax.broadcasted_iota(jnp.int32, (TILE, count * part), 1) + (base + first * part)
    bias = jnp.where(at_key.astype(jnp.float32) >= starts_ref[row : row + TILE, 0:1], 0.0, MASKED)
    for group in range(GROUPS):
        heads = pl.ds(group * PER, PER)
        raw = score(query_tile(q_ref, group, row), chunk(kv_ref, 0, group, first, count), bias)
        old = top_ref[heads, row : row + TILE]
        top = jnp.maximum(old, jnp.max(raw, axis=2, keepdims=True))
        summed = weigh(raw, top[:, :, 0:1], chunk(kv_ref, 1, group, first, count))
        keep = jnp.exp2((old - top) * SCALE)
        yield heads, row, top, (
            acc_ref[heads, row : row + TILE] * keep + summed[:, :, :HD],
            sum_ref[heads, row : row + TILE] * keep + summed[:, :, HD:],
        )


def near_kernel(q_ref, kv_ref, starts_ref, acc_in, sum_in, top_in, acc_ref, sum_ref, top_ref):
    rows = q_ref.shape[0]
    chip = lax.div(lax.axis_index("ctx"), CORES)
    base = (chip - 1) * CORES * rows
    for tile in range(rows // TILE):
        parts = update(
            q_ref, kv_ref, starts_ref, (acc_in, sum_in, top_in), tile, base, 0, kv_ref.shape[0]
        )
        for heads, row, top, (acc, total) in parts:
            acc_ref[heads, row : row + TILE] = acc
            sum_ref[heads, row : row + TILE] = total
            top_ref[heads, row : row + TILE] = top


def far_kernel(q_ref, kv_ref, starts_ref, acc_in, sum_in, top_in, out_ref):
    rows = q_ref.shape[0]
    blocks, part = kv_ref.shape[0], kv_ref.shape[3]
    chip = lax.div(lax.axis_index("ctx"), CORES)
    base = (chip - 2) * CORES * rows
    end = (base + CORES * rows).astype(jnp.float32)

    def write(heads, row, acc, total):
        result = (acc / total).astype(out_ref.dtype)
        for j in range(PER):
            column = (heads.start + j) * HD
            out_ref[row : row + TILE, column : column + HD] = result[j]

    for tile in range(rows // TILE):
        row = tile * TILE
        needed = end - jnp.min(starts_ref[row : row + 8])
        steps = [0, blocks // 2, blocks]
        for low, high in zip(steps[:-1], steps[1:]):

            @pl.when((needed > low * part) & (needed <= high * part))
            def _():
                parts = update(
                    q_ref, kv_ref, starts_ref, (acc_in, sum_in, top_in), tile, base,
                    blocks - high, high,
                )
                for heads, row, _, (acc, total) in parts:
                    write(heads, row, acc, total)

        @pl.when(needed <= 0)
        def _():
            for group in range(GROUPS):
                heads = pl.ds(group * PER, PER)
                write(heads, row, acc_in[heads, row : row + TILE], sum_in[heads, row : row + TILE])


def cost(rows, keys):
    pairs = rows * keys * HEADS
    return pl.CostEstimate(
        flops=pairs * HD * 6, bytes_accessed=8 * rows * HEADS * HD, transcendentals=pairs
    )


def local(queries, keys, values, doc_lengths):
    rows = queries.shape[0]
    targets = lax.axis_size("head")
    packed = pack(keys, values, targets)
    own = lax.all_to_all(packed, "head", split_axis=0, concat_axis=0, tiled=True)
    first = shifted(own, CORES)
    own_both = both_cores(own)
    state = [jax.ShapeDtypeStruct((HEADS, rows, HD), jnp.float32)] * 3
    params = pltpu.CompilerParams(vmem_limit_bytes=VMEM)
    starts, *carried = pl.pallas_call(
        own_kernel,
        out_shape=[jax.ShapeDtypeStruct((rows, HD), jnp.float32)] + state,
        compiler_params=params,
        cost_estimate=cost(rows, 2 * rows),
        name="own",
    )(doc_lengths.reshape(1, -1), queries, own_both)
    second = shifted(first, CORES)
    first_both = both_cores(first)
    carried = pl.pallas_call(
        near_kernel,
        out_shape=state,
        compiler_params=params,
        cost_estimate=cost(rows, 2 * rows),
        name="near",
    )(queries, first_both, starts, *carried)
    second_both = both_cores(second)
    return pl.pallas_call(
        far_kernel,
        out_shape=jax.ShapeDtypeStruct(queries.shape, queries.dtype),
        compiler_params=params,
        cost_estimate=cost(rows, rows),
        name="far",
    )(queries, second_both, starts, *carried)


def solution(mesh):
    placed = (P("ctx", "head"), P(("ctx", "head"), None), P(("ctx", "head"), None), P())
    return jax.shard_map(
        local, mesh=mesh, in_specs=placed, out_specs=P("ctx", "head"), check_vma=False
    )
```

time: 101 us -> 51.2 us (0.51)
  the two profiles are of different devices: /device:TPU:351 before, /device:TPU:248 now
where the time goes in v1:
time: 51.2 us; the launch traced here: 51 us
  blocking collectives  19.5 us (38%)
  Pallas kernels  14.3 us (28%)
  starting transfers between devices  12.4 us (24%)
  waiting for transfers between devices  4.79 us (9%)
    ppermute x2, starting transfers between devices, shifted(): lax.ppermute(value, 'ctx', [(at, at + steps) for at in range(count - step...  12.4 us
    all_to_all x1, blocking collectives, local(): lax.all_to_all(packed, 'head', split_axis=0, concat_axis=0, tiled=True)  12.4 us
    all_gather x3, blocking collectives, both_cores(): lax.all_gather(value, 'ctx', axis=0, tiled=True, axis_index_groups=pairs)  7.11 us
    pallas_call x1, Pallas kernels, local(): pl.pallas_call(far_kernel, out_shape=jax.ShapeDtypeStruct(queries.shape,...  5.32 us
    ppermute x2, waiting for transfers between devices, shifted(): lax.ppermute(value, 'ctx', [(at, at + steps) for at in range(count - step...  4.79 us
    pallas_call x1, Pallas kernels, local(): pl.pallas_call(near_kernel, out_shape=state, compiler_params=params, cost...  4.16 us
    pallas_call x1, Pallas kernels, local(): pl.pallas_call(own_kernel, out_shape=[jax.ShapeDtypeStruct((rows, HD), jn...  2.91 us
    pallas_call x1, Pallas kernels, pack(): pl.pallas_call(pack_kernel, out_shape=jax.ShapeDtypeStruct((targets, 2, G...  1.91 us
  transfers between devices with their start and end apart: 2, of which 1 were waited for; matrix products, arithmetic and copies ran while one was open for 0% of the time, Pallas kernels for 14%

profile of v1, /device:TPU:248, one launch (start us, length us, event | category | flops | bytes accessed | tf_op | source)
XLA Modules:
  0.0 51.0 jit_solution(3350991516487594773)
XLA Ops:
  0.0 0.0 copy-start.1
  0.0 0.0 copy-start
  0.0 1.9 %pack.1 = bf16[4,2,2,96,128]{4,3,2,1,0:T(8,128)(2,1)} custom-call(bf16[96,1024]{1,0:T(8,128)(2,1)} %k_ref.1, bf16[96,1024]{1,0:T(8,128)(2,1)} %v_ref.1), custom_call_target="tpu_custom_call" | custom-call | tf_op jit(solution)/shard_map/pack/pallas_call | solution.py:42
  1.9 12.4 %all_to_all.5 = bf16[4,2,2,96,128]{4,3,2,1,0:T(8,128)(2,1)S(1)} all-to-all(bf16[4,2,2,96,128]{4,3,2,1,0:T(8,128)(2,1)} %pack.1), channel_id=1, replica_groups=mesh['ctx'=128,'head'=4] {'head'}, dimensions={0} | all-to-all | bytes 786432 | tf_op jit(solution)/shard_map/all_to_all | solution.py:213
  14.3 4.7 %collective-permute-start = (bf16[4,2,2,96,128]{4,3,2,1,0:T(8,128)(2,1)S(1)}, bf16[4,2,2,96,128]{4,3,2,1,0:T(8,128)(2,1)S(1)}, u32[]{:S(2)}, u32[]{:S(2)}) collective-permute-start(bf16[4,2,2,96,128]{4,3,2,1,0:T(8,128)(2,1)S(1)} %all_to_all.5), channel_id=1, source_target_pairs={{0,8},{4,12},{8,16},{12,20},{16,24},{20,28},{24,32},{28,36},{32,40... | collective-permute-start | bytes 1179656 | tf_op jit(solution)/shard_map/ppermute | solution.py:24
  19.0 2.4 %all_gather.10.kv_ref = bf16[8,2,2,96,128]{4,3,2,1,0:T(8,128)(2,1)S(1)} all-gather(bf16[4,2,2,96,128]{4,3,2,1,0:T(8,128)(2,1)S(1)} %all_to_all.5), channel_id=1, replica_groups={{0,4},{8,12},{16,20},{24,28},{32,36},{40,44},{48,52},{56,60},{64,68},{7..., dimensions={0}, use_global_device_ids=true | all-gather | bytes 1179648 | tf_op jit(solution)/shard_map/all_gather | solution.py:30
  21.3 4.8 %collective-permute-done = bf16[4,2,2,96,128]{4,3,2,1,0:T(8,128)(2,1)S(1)} collective-permute-done((bf16[4,2,2,96,128]{4,3,2,1,0:T(8,128)(2,1)S(1)}, bf16[4,2,2,96,128]{4,3,2,1,0:T(8,128)(2,1)S(1)}, u32[]{:S(2)}, u32[]{:S(2)}) %collective-permute-start) | collective-permute-done | bytes 393248 | tf_op jit(solution)/shard_map/ppermute | solution.py:24
  26.1 7.7 %collective-permute-start.1 = (bf16[4,2,2,96,128]{4,3,2,1,0:T(8,128)(2,1)S(1)}, bf16[4,2,2,96,128]{4,3,2,1,0:T(8,128)(2,1)S(1)}, u32[]{:S(2)}, u32[]{:S(2)}) collective-permute-start(bf16[4,2,2,96,128]{4,3,2,1,0:T(8,128)(2,1)S(1)} %collective-permute-done), channel_id=1, source_target_pairs={{0,8},{4,12},{8,16},{12,20},{16,24},{20,28},{24,32},{28,36},{32,40... | collective-permute-start | bytes 1179656 | tf_op jit(solution)/shard_map/ppermute | solution.py:24
  33.8 0.0 copy-done.1
  33.8 0.0 copy-done
  33.9 2.9 %own.1 = (f32[384,128]{1,0:T(8,128)S(1)}, f32[8,384,128]{2,1,0:T(8,128)S(1)}, f32[8,384,128]{2,1,0:T(8,128)S(1)}, f32[8,384,128]{2,1,0:T(8,128)S(1)}) custom-call(s32[1,512]{1,0:T(1,128)S(1)} %bitcast.1, bf16[384,1024]{1,0:T(8,128)(2,1)S(1)} %copy-done, bf16[8,2,2,96,128]{4,3,2,1,0:T(8,128)(2,1)S(1)} %all_gather.10.kv_ref), custom_call_target="tpu_custom_call" | custom-call | flops 1811939328 | bytes 3145728 | tf_op jit(solution)/shard_map/own/pallas_call | solution.py:218
  36.8 2.4 %all_gather.11.kv_ref = bf16[8,2,2,96,128]{4,3,2,1,0:T(8,128)(2,1)S(1)} all-gather(bf16[4,2,2,96,128]{4,3,2,1,0:T(8,128)(2,1)S(1)} %collective-permute-done), channel_id=1, replica_groups={{0,4},{8,12},{16,20},{24,28},{32,36},{40,44},{48,52},{56,60},{64,68},{7..., dimensions={0}, use_global_device_ids=true | all-gather | bytes 1179648 | tf_op jit(solution)/shard_map/all_gather | solution.py:30
  39.1 4.2 %near.1 = (f32[8,384,128]{2,1,0:T(8,128)S(1)}, f32[8,384,128]{2,1,0:T(8,128)S(1)}, f32[8,384,128]{2,1,0:T(8,128)S(1)}) custom-call(bf16[384,1024]{1,0:T(8,128)(2,1)S(1)} %copy-done, bf16[8,2,2,96,128]{4,3,2,1,0:T(8,128)(2,1)S(1)} %all_gather.11.kv_ref, f32[384,128]{1,0:T(8,128)S(1)} %get-tuple-element.12.starts_ref, ...), custom_call_target="tpu_custom_call" | custom-call | flops 1811939328 | bytes 3145728 | tf_op jit(solution)/shard_map/near/pallas_call | solution.py:227
  43.3 0.0 collective-permute-done.1
  43.3 2.4 %all_gather.9.kv_ref = bf16[8,2,2,96,128]{4,3,2,1,0:T(8,128)(2,1)S(1)} all-gather(bf16[4,2,2,96,128]{4,3,2,1,0:T(8,128)(2,1)S(1)} %collective-permute-done.1), channel_id=1, replica_groups={{0,4},{8,12},{16,20},{24,28},{32,36},{40,44},{48,52},{56,60},{64,68},{7..., dimensions={0}, use_global_device_ids=true | all-gather | bytes 1179648 | tf_op jit(solution)/shard_map/all_gather | solution.py:30
  45.7 5.3 %far.1 = bf16[384,1024]{1,0:T(8,128)(2,1)} custom-call(bf16[384,1024]{1,0:T(8,128)(2,1)S(1)} %copy-done, bf16[8,2,2,96,128]{4,3,2,1,0:T(8,128)(2,1)S(1)} %all_gather.9.kv_ref, f32[384,128]{1,0:T(8,128)S(1)} %get-tuple-element.12.starts_ref, f32[8,384,128]{2,1,0:T(8,128)S(1)} %get-tuple-element.16.acc_in, f32[8,384,128]{2,1,0:T(8,128)S(1)} %get-tuple-element.17.sum_in, ...), custom_call_target="tpu_custom_call" | custom-call | flops 905969664 | bytes 3145728 | tf_op jit(solution)/shard_map/far/pallas_call | solution.py:235
Async XLA Ops:
  0.0 33.8 %copy-start.1 = (s32[512]{0:T(512)S(1)}, s32[512]{0:T(512)}, u32[]{:S(2)}) copy-start(s32[512]{0:T(512)} %param.7) | copy-start | bytes 6148
  0.0 33.8 %copy-start = (bf16[384,1024]{1,0:T(8,128)(2,1)S(1)}, bf16[384,1024]{1,0:T(8,128)(2,1)}, u32[]{:S(2)}) copy-start(bf16[384,1024]{1,0:T(8,128)(2,1)} %q_ref.5) | copy-start | bytes 2359300
  14.3 11.9 %collective-permute-start = (bf16[4,2,2,96,128]{4,3,2,1,0:T(8,128)(2,1)S(1)}, bf16[4,2,2,96,128]{4,3,2,1,0:T(8,128)(2,1)S(1)}, u32[]{:S(2)}, u32[]{:S(2)}) collective-permute-start(bf16[4,2,2,96,128]{4,3,2,1,0:T(8,128)(2,1)S(1)} %all_to_all.5), channel_id=1, source_target_pairs={{0,8},{4,12},{8,16},{12,20},{16,24},{20,28},{24,32},{28,36},{32,40... | collective-permute-start | bytes 1179656 | tf_op jit(solution)/shard_map/ppermute | solution.py:24
  26.1 17.2 %collective-permute-start.1 = (bf16[4,2,2,96,128]{4,3,2,1,0:T(8,128)(2,1)S(1)}, bf16[4,2,2,96,128]{4,3,2,1,0:T(8,128)(2,1)S(1)}, u32[]{:S(2)}, u32[]{:S(2)}) collective-permute-start(bf16[4,2,2,96,128]{4,3,2,1,0:T(8,128)(2,1)S(1)} %collective-permute-done), channel_id=1, source_target_pairs={{0,8},{4,12},{8,16},{12,20},{16,24},{20,28},{24,32},{28,36},{32,40... | collective-permute-start | bytes 1179656 | tf_op jit(solution)/shard_map/ppermute | solution.py:24

commit v2 on v1

v2 whole, which is shorter than its diff:
```python
import functools
import math

import jax
import jax.numpy as jnp
from jax import lax
from jax.experimental import pallas as pl
from jax.experimental.pallas import tpu as pltpu
from jax.sharding import PartitionSpec as P

HD = 128
GROUPS = 2
PER = 4
HEADS = GROUPS * PER
CORES = 2
MASKED = -1e30
TILE = 128
STEP = 256
SCALE = math.log2(math.e) / math.sqrt(HD)
VMEM = 40 * 1024 * 1024


def shifted(value, steps):
    count = lax.axis_size("ctx")
    return lax.ppermute(value, "ctx", [(at, at + steps) for at in range(count - steps)])


def both_cores(value):
    count = lax.axis_size("ctx")
    pairs = [[at + core for core in range(CORES)] for at in range(0, count, CORES)]
    return lax.all_gather(value, "ctx", axis=0, tiled=True, axis_index_groups=pairs)


def pack_kernel(k_ref, v_ref, out_ref):
    for kind, ref in enumerate((k_ref, v_ref)):
        for column in range(out_ref.shape[0] * GROUPS):
            part = ref[:, column * HD : (column + 1) * HD]
            out_ref[column // GROUPS, kind, column % GROUPS] = part


def pack(keys, values, targets):
    rows = keys.shape[0]
    return pl.pallas_call(
        pack_kernel,
        out_shape=jax.ShapeDtypeStruct((targets, 2, GROUPS, rows, HD), keys.dtype),
        name="pack",
    )(keys, values)


def chunk(kv_ref, kind, group, first, count):
    blocks, part = kv_ref.shape[0], kv_ref.shape[3]
    return kv_ref[:, kind, group].reshape(blocks * part, HD)[first : first + count]


def with_ones(values):
    return jnp.concatenate([values, jnp.ones_like(values)], axis=1)


def stacked(q_ref, group, rows):
    heads = range(group * PER, (group + 1) * PER)
    return jnp.concatenate([q_ref[rows, head * HD : (head + 1) * HD] for head in heads], axis=0)


def score(queries, keys):
    raw = lax.dot_general(
        queries, keys, (((1,), (1,)), ((), ())), preferred_element_type=jnp.float32
    )
    return raw.reshape(PER, TILE, keys.shape[0])


def weigh(raw, top):
    return jnp.exp2((raw - top) * SCALE).astype(jnp.bfloat16)


def total(weights, values):
    flat = weights.reshape(PER * TILE, values.shape[0])
    summed = jnp.dot(flat, with_ones(values), preferred_element_type=jnp.float32)
    return summed.reshape(PER, TILE, 2 * HD)


def doc_starts(lengths_ref, starts_ref, first):
    lengths = lengths_ref[...]
    docs = lengths.shape[1]
    earlier = lax.broadcasted_iota(jnp.int32, (docs, docs), 0) < lax.broadcasted_iota(
        jnp.int32, (docs, docs), 1
    )
    earlier = earlier.astype(jnp.bfloat16)

    def before(part):
        part = jnp.broadcast_to(part.astype(jnp.float32), (16, docs)).astype(jnp.bfloat16)
        return jnp.dot(part, earlier, preferred_element_type=jnp.float32)[0:1]

    begins = before(lengths >> 4) * 16.0 + before(lengths & 15)
    rows = starts_ref.shape[0]
    for row in range(0, rows, TILE):
        at = lax.broadcasted_iota(jnp.int32, (TILE, docs), 0) + (first + row)
        at = at.astype(jnp.float32)
        found = jnp.max(jnp.where(begins <= at, begins, 0.0), axis=1, keepdims=True)
        starts_ref[row : row + TILE] = jnp.broadcast_to(found, (TILE, HD))


def own_kernel(q_ref, kv_ref, lengths_ref, starts_ref, acc_ref, sum_ref, top_ref):
    rows = q_ref.shape[0]
    device = lax.axis_index("ctx")
    core = lax.rem(device, CORES)
    doc_starts(lengths_ref, starts_ref, device * rows)

    def run(earlier):
        for tile in range(rows // TILE):
            row = tile * TILE
            keys = -(-(row + TILE + earlier * rows) // STEP) * STEP
            at_key = lax.broadcasted_iota(jnp.int32, (TILE, keys), 1) - earlier * rows
            at_query = lax.broadcasted_iota(jnp.int32, (TILE, keys), 0) + row
            since = starts_ref[row : row + TILE, 0:1] - (device * rows).astype(jnp.float32)
            allowed = (at_key <= at_query) & (at_key.astype(jnp.float32) >= since)
            bias = jnp.where(allowed, 0.0, MASKED)
            raws, sums = [], []
            for group in range(GROUPS):
                queries = stacked(q_ref, group, pl.ds(row, TILE))
                raws.append(score(queries, chunk(kv_ref, 0, group, 0, keys)) + bias[None])
            tops = [jnp.max(raw, axis=2, keepdims=True) for raw in raws]
            weights = [weigh(raw, top) for raw, top in zip(raws, tops)]
            for group, part in enumerate(weights):
                sums.append(total(part, chunk(kv_ref, 1, group, 0, keys)))
            for group in range(GROUPS):
                heads = pl.ds(group * PER, PER)
                acc_ref[heads, row : row + TILE] = sums[group][:, :, :HD]
                sum_ref[heads, row : row + TILE] = sums[group][:, :, HD:]
                top_ref[heads, row : row + TILE] = jnp.broadcast_to(tops[group], (PER, TILE, HD))

    for which in range(CORES):
        pl.when(core == which)(functools.partial(run, which))


def update(q_ref, kv_ref, starts_ref, state, row, base, first, count):
    acc_ref, sum_ref, top_ref = state
    rows = pl.ds(row, TILE)
    at_key = lax.broadcasted_iota(jnp.int32, (TILE, count), 1) + (base + first)
    bias = jnp.where(at_key.astype(jnp.float32) >= starts_ref[rows, 0:1], 0.0, MASKED)
    raws, tops, sums = [], [], []
    for group in range(GROUPS):
        keys = chunk(kv_ref, 0, group, first, count)
        raws.append(score(stacked(q_ref, group, rows), keys) + bias[None])
    for group, raw in enumerate(raws):
        old = top_ref[pl.ds(group * PER, PER), rows]
        tops.append(jnp.maximum(old, jnp.max(raw, axis=2, keepdims=True)))
    weights = [weigh(raw, top[:, :, 0:1]) for raw, top in zip(raws, tops)]
    for group, part in enumerate(weights):
        sums.append(total(part, chunk(kv_ref, 1, group, first, count)))
    for head in range(HEADS):
        group, j = divmod(head, PER)
        keep = jnp.exp2((top_ref[head, rows] - tops[group][j]) * SCALE)
        acc = acc_ref[head, rows] * keep + sums[group][j][:, :HD]
        yield head, tops[group][j], acc, sum_ref[head, rows] * keep + sums[group][j][:, HD:]


def near_kernel(q_ref, kv_ref, starts_ref, acc_in, sum_in, top_in, acc_ref, sum_ref, top_ref):
    rows = q_ref.shape[0]
    chip = lax.div(lax.axis_index("ctx"), CORES)
    base = (chip - 1) * CORES * rows
    state = (acc_in, sum_in, top_in)
    @pl.loop(0, rows // TILE)
    def _(tile):
        row = pl.multiple_of(tile * TILE, TILE)
        parts = update(q_ref, kv_ref, starts_ref, state, row, base, 0, CORES * rows)
        for head, top, acc, summed in parts:
            acc_ref[head, pl.ds(row, TILE)] = acc
            sum_ref[head, pl.ds(row, TILE)] = summed
            top_ref[head, pl.ds(row, TILE)] = top


def far_kernel(q_ref, kv_ref, starts_ref, acc_in, sum_in, top_in, out_ref):
    rows = q_ref.shape[0]
    tiles = rows // TILE
    chip = lax.div(lax.axis_index("ctx"), CORES)
    base = (chip - 2) * CORES * rows
    end = (base + CORES * rows).astype(jnp.float32)
    state = (acc_in, sum_in, top_in)
    since = [jnp.min(starts_ref[tile * TILE : tile * TILE + 8]) for tile in range(tiles)]
    reaching = [(start < end).astype(jnp.int32) for start in since]
    reaching = functools.reduce(lambda one, two: one + two, reaching)
    needed = end - since[0]

    def write(head, row, acc, total):
        rough = pl.reciprocal(total, approx=True)
        result = acc * (rough * (2.0 - total * rough))
        out_ref[pl.ds(row, TILE), head * HD : (head + 1) * HD] = result.astype(out_ref.dtype)

    def finish(tile):
        row = pl.multiple_of(tile * TILE, TILE)
        for head in range(HEADS):
            write(head, row, acc_in[head, pl.ds(row, TILE)], sum_in[head, pl.ds(row, TILE)])

    def reach(used, tile):
        row = pl.multiple_of(tile * TILE, TILE)
        parts = update(q_ref, kv_ref, starts_ref, state, row, base, CORES * rows - used, used)
        for head, _, acc, total in parts:
            write(head, row, acc, total)

    for low in range(0, CORES * rows, STEP):
        inside = (needed > low) & (needed <= low + STEP)

        @pl.when(inside)
        def _():
            pl.loop(0, reaching)(functools.partial(reach, low + STEP))

    pl.loop(reaching, tiles)(finish)


def cost(rows, keys):
    pairs = rows * keys * HEADS
    return pl.CostEstimate(
        flops=pairs * HD * 6, bytes_accessed=8 * rows * HEADS * HD, transcendentals=pairs
    )


def call(kernel, name, out_shape, keys, *operands):
    rows = operands[0].shape[0]
    return pl.pallas_call(
        kernel,
        out_shape=out_shape,
        compiler_params=pltpu.CompilerParams(vmem_limit_bytes=VMEM),
        cost_estimate=cost(rows, keys),
        name=name,
    )(*operands)


def own_part(queries, kv, doc_lengths):
    rows = queries.shape[0]
    state = [jax.ShapeDtypeStruct((HEADS, rows, HD), jnp.float32)] * 3
    starts = jax.ShapeDtypeStruct((rows, HD), jnp.float32)
    return call(
        own_kernel, "own", [starts] + state, 2 * rows, queries, kv, doc_lengths.reshape(1, -1)
    )


def near_part(queries, kv, starts, *state):
    shapes = [jax.ShapeDtypeStruct(part.shape, part.dtype) for part in state]
    return call(near_kernel, "near", shapes, kv.shape[0] * kv.shape[3], queries, kv, starts, *state)


def far_part(queries, kv, starts, *state):
    out = jax.ShapeDtypeStruct(queries.shape, queries.dtype)
    return call(far_kernel, "far", out, queries.shape[0], queries, kv, starts, *state)


def attention(queries, own_both, first_both, second_both, doc_lengths):
    starts, *state = own_part(queries, own_both, doc_lengths)
    state = near_part(queries, first_both, starts, *state)
    return far_part(queries, second_both, starts, *state)


def local(queries, keys, values, doc_lengths):
    targets = lax.axis_size("head")
    packed = pack(keys, values, targets)
    own = lax.all_to_all(packed, "head", split_axis=0, concat_axis=0, tiled=True)
    first = shifted(own, CORES)
    starts, *state = own_part(queries, both_cores(own), doc_lengths)
    first, starts = lax.optimization_barrier((first, starts))
    second = shifted(first, CORES)
    state = near_part(queries, both_cores(first), starts, *state)
    return far_part(queries, both_cores(second), starts, *state)


def solution(mesh):
    placed = (P("ctx", "head"), P(("ctx", "head"), None), P(("ctx", "head"), None), P())
    return jax.shard_map(
        local, mesh=mesh, in_specs=placed, out_specs=P("ctx", "head"), check_vma=False
    )
```

time: 51.2 us -> 47.4 us (0.926)
  the two profiles are of different devices: /device:TPU:248 before, /device:TPU:320 now
where the time goes in v2:
time: 47.4 us; the launch traced here: 47.2 us
  blocking collectives  19.5 us (41%)
  Pallas kernels  12.6 us (27%)
  waiting for transfers between devices  9.75 us (21%)
  starting transfers between devices  5.38 us (11%)
    all_to_all x1, blocking collectives, local(): lax.all_to_all(packed, 'head', split_axis=0, concat_axis=0, tiled=True)  12.4 us
    pallas_call x3, Pallas kernels, call(): pl.pallas_call(kernel, out_shape=out_shape, compiler_params=pltpu.Compile...  10.7 us
    ppermute x2, waiting for transfers between devices, shifted(): lax.ppermute(value, 'ctx', [(at, at + steps) for at in range(count - step...  9.75 us
    all_gather x3, blocking collectives, both_cores(): lax.all_gather(value, 'ctx', axis=0, tiled=True, axis_index_groups=pairs)  7.09 us
    ppermute x2, starting transfers between devices, shifted(): lax.ppermute(value, 'ctx', [(at, at + steps) for at in range(count - step...  5.38 us
    pallas_call x1, Pallas kernels, pack(): pl.pallas_call(pack_kernel, out_shape=jax.ShapeDtypeStruct((targets, 2, G...  1.91 us
  transfers between devices with their start and end apart: 2, of which 2 were waited for; matrix products, arithmetic and copies ran while one was open for 0% of the time, Pallas kernels for 14%

profile of v2, /device:TPU:320, one launch (start us, length us, event | category | flops | bytes accessed | tf_op | source)
XLA Modules:
  0.0 47.2 jit_solution(3245867724048598189)
XLA Ops:
  0.0 0.0 copy-start.1
  0.0 0.0 copy-start
  0.0 1.9 %pack.1 = bf16[4,2,2,96,128]{4,3,2,1,0:T(8,128)(2,1)} custom-call(bf16[96,1024]{1,0:T(8,128)(2,1)} %k_ref.1, bf16[96,1024]{1,0:T(8,128)(2,1)} %v_ref.1), custom_call_target="tpu_custom_call" | custom-call | tf_op jit(solution)/shard_map/pack/pallas_call | solution.py:43
  1.9 12.4 %all_to_all.5 = bf16[4,2,2,96,128]{4,3,2,1,0:T(8,128)(2,1)S(1)} all-to-all(bf16[4,2,2,96,128]{4,3,2,1,0:T(8,128)(2,1)} %pack.1), channel_id=1, replica_groups=mesh['ctx'=128,'head'=4] {'head'}, dimensions={0} | all-to-all | bytes 786432 | tf_op jit(solution)/shard_map/all_to_all | solution.py:256
  14.3 3.5 %collective-permute-start = (bf16[4,2,2,96,128]{4,3,2,1,0:T(8,128)(2,1)S(1)}, bf16[4,2,2,96,128]{4,3,2,1,0:T(8,128)(2,1)S(1)}, u32[]{:S(2)}, u32[]{:S(2)}) collective-permute-start(bf16[4,2,2,96,128]{4,3,2,1,0:T(8,128)(2,1)S(1)} %all_to_all.5), channel_id=1, source_target_pairs={{0,8},{4,12},{8,16},{12,20},{16,24},{20,28},{24,32},{28,36},{32,40... | collective-permute-start | bytes 1179656 | tf_op jit(solution)/shard_map/ppermute | solution.py:25
  17.8 2.4 %all_gather.9.kv_ref = bf16[8,2,2,96,128]{4,3,2,1,0:T(8,128)(2,1)S(1)} all-gather(bf16[4,2,2,96,128]{4,3,2,1,0:T(8,128)(2,1)S(1)} %all_to_all.5), channel_id=1, replica_groups={{0,4},{8,12},{16,20},{24,28},{32,36},{40,44},{48,52},{56,60},{64,68},{7..., dimensions={0}, use_global_device_ids=true | all-gather | bytes 1179648 | tf_op jit(solution)/shard_map/all_gather | solution.py:31
  20.1 0.0 copy-done.1
  20.1 0.0 copy-done
  20.1 2.0 %own.1 = (f32[384,128]{1,0:T(8,128)S(1)}, f32[8,384,128]{2,1,0:T(8,128)S(1)}, f32[8,384,128]{2,1,0:T(8,128)S(1)}, f32[8,384,128]{2,1,0:T(8,128)S(1)}) custom-call(bf16[384,1024]{1,0:T(8,128)(2,1)S(1)} %copy-done, bf16[8,2,2,96,128]{4,3,2,1,0:T(8,128)(2,1)S(1)} %all_gather.9.kv_ref, s32[1,512]{1,0:T(1,128)S(1)} %bitcast.1), custom_call_target="tpu_custom_call" | custom-call | flops 1811939328 | bytes 3145728 | tf_op jit(solution)/shard_map/own/pallas_call | solution.py:219
  22.1 5.8 %collective-permute-done = bf16[4,2,2,96,128]{4,3,2,1,0:T(8,128)(2,1)S(1)} collective-permute-done((bf16[4,2,2,96,128]{4,3,2,1,0:T(8,128)(2,1)S(1)}, bf16[4,2,2,96,128]{4,3,2,1,0:T(8,128)(2,1)S(1)}, u32[]{:S(2)}, u32[]{:S(2)}) %collective-permute-start) | collective-permute-done | bytes 393248 | tf_op jit(solution)/shard_map/ppermute | solution.py:25
  27.9 1.9 %collective-permute-start.1 = (bf16[4,2,2,96,128]{4,3,2,1,0:T(8,128)(2,1)S(1)}, bf16[4,2,2,96,128]{4,3,2,1,0:T(8,128)(2,1)S(1)}, u32[]{:S(2)}, u32[]{:S(2)}) collective-permute-start(bf16[4,2,2,96,128]{4,3,2,1,0:T(8,128)(2,1)S(1)} %collective-permute-done), channel_id=1, source_target_pairs={{0,8},{4,12},{8,16},{12,20},{16,24},{20,28},{24,32},{28,36},{32,40... | collective-permute-start | bytes 1179656 | tf_op jit(solution)/shard_map/ppermute | solution.py:25
  29.9 2.4 %all_gather.11.kv_ref = bf16[8,2,2,96,128]{4,3,2,1,0:T(8,128)(2,1)S(1)} all-gather(bf16[4,2,2,96,128]{4,3,2,1,0:T(8,128)(2,1)S(1)} %collective-permute-done), channel_id=1, replica_groups={{0,4},{8,12},{16,20},{24,28},{32,36},{40,44},{48,52},{56,60},{64,68},{7..., dimensions={0}, use_global_device_ids=true | all-gather | bytes 1179648 | tf_op jit(solution)/shard_map/all_gather | solution.py:31
  32.2 4.5 %near.1 = (f32[8,384,128]{2,1,0:T(8,128)S(1)}, f32[8,384,128]{2,1,0:T(8,128)S(1)}, f32[8,384,128]{2,1,0:T(8,128)S(1)}) custom-call(bf16[384,1024]{1,0:T(8,128)(2,1)S(1)} %copy-done, bf16[8,2,2,96,128]{4,3,2,1,0:T(8,128)(2,1)S(1)} %all_gather.11.kv_ref, f32[384,128]{1,0:T(8,128)S(1)} %get-tuple-element.16.starts_ref, ...), custom_call_target="tpu_custom_call" | custom-call | flops 1811939328 | bytes 3145728 | tf_op jit(solution)/shard_map/near/pallas_call | solution.py:219
  36.7 4.0 %collective-permute-done.1 = bf16[4,2,2,96,128]{4,3,2,1,0:T(8,128)(2,1)S(1)} collective-permute-done((bf16[4,2,2,96,128]{4,3,2,1,0:T(8,128)(2,1)S(1)}, bf16[4,2,2,96,128]{4,3,2,1,0:T(8,128)(2,1)S(1)}, u32[]{:S(2)}, u32[]{:S(2)}) %collective-permute-start.1) | collective-permute-done | bytes 393248 | tf_op jit(solution)/shard_map/ppermute | solution.py:25
  40.7 2.4 %all_gather.10.kv_ref = bf16[8,2,2,96,128]{4,3,2,1,0:T(8,128)(2,1)S(1)} all-gather(bf16[4,2,2,96,128]{4,3,2,1,0:T(8,128)(2,1)S(1)} %collective-permute-done.1), channel_id=1, replica_groups={{0,4},{8,12},{16,20},{24,28},{32,36},{40,44},{48,52},{56,60},{64,68},{7..., dimensions={0}, use_global_device_ids=true | all-gather | bytes 1179648 | tf_op jit(solution)/shard_map/all_gather | solution.py:31
  43.0 4.2 %far.1 = bf16[384,1024]{1,0:T(8,128)(2,1)} custom-call(bf16[384,1024]{1,0:T(8,128)(2,1)S(1)} %copy-done, bf16[8,2,2,96,128]{4,3,2,1,0:T(8,128)(2,1)S(1)} %all_gather.10.kv_ref, f32[384,128]{1,0:T(8,128)S(1)} %get-tuple-element.16.starts_ref, f32[8,384,128]{2,1,0:T(8,128)S(1)} %get-tuple-element.20.acc_in, f32[8,384,128]{2,1,0:T(8,128)S(1)} %get-tuple-element.21.sum_in, ...), custom_call_target="tpu_custom_call" | custom-call | flops 905969664 | bytes 3145728 | tf_op jit(solution)/shard_map/far/pallas_call | solution.py:219
Async XLA Ops:
  0.0 20.1 %copy-start.1 = (s32[512]{0:T(512)S(1)}, s32[512]{0:T(512)}, u32[]{:S(2)}) copy-start(s32[512]{0:T(512)} %param.7) | copy-start | bytes 6148
  0.0 20.1 %copy-start = (bf16[384,1024]{1,0:T(8,128)(2,1)S(1)}, bf16[384,1024]{1,0:T(8,128)(2,1)}, u32[]{:S(2)}) copy-start(bf16[384,1024]{1,0:T(8,128)(2,1)} %q_ref.5) | copy-start | bytes 2359300
  14.3 13.7 %collective-permute-start = (bf16[4,2,2,96,128]{4,3,2,1,0:T(8,128)(2,1)S(1)}, bf16[4,2,2,96,128]{4,3,2,1,0:T(8,128)(2,1)S(1)}, u32[]{:S(2)}, u32[]{:S(2)}) collective-permute-start(bf16[4,2,2,96,128]{4,3,2,1,0:T(8,128)(2,1)S(1)} %all_to_all.5), channel_id=1, source_target_pairs={{0,8},{4,12},{8,16},{12,20},{16,24},{20,28},{24,32},{28,36},{32,40... | collective-permute-start | bytes 1179656 | tf_op jit(solution)/shard_map/ppermute | solution.py:25
  27.9 12.7 %collective-permute-start.1 = (bf16[4,2,2,96,128]{4,3,2,1,0:T(8,128)(2,1)S(1)}, bf16[4,2,2,96,128]{4,3,2,1,0:T(8,128)(2,1)S(1)}, u32[]{:S(2)}, u32[]{:S(2)}) collective-permute-start(bf16[4,2,2,96,128]{4,3,2,1,0:T(8,128)(2,1)S(1)} %collective-permute-done), channel_id=1, source_target_pairs={{0,8},{4,12},{8,16},{12,20},{16,24},{20,28},{24,32},{28,36},{32,40... | collective-permute-start | bytes 1179656 | tf_op jit(solution)/shard_map/ppermute | solution.py:25

commit v3 on v2

--- a/solution.py
+++ b/solution.py
@@ -31,25 +31,51 @@
     return lax.all_gather(value, "ctx", axis=0, tiled=True, axis_index_groups=pairs)
 
 
-def pack_kernel(k_ref, v_ref, out_ref):
+def moved(value, steps, turn):
+    chips, heads = lax.axis_size("ctx") // CORES, lax.axis_size("head")
+    pairs = [
+        ((chip * CORES + core) * heads + head,
+         ((chip + steps) * CORES + core) * heads + (head + turn(core)) % heads)
+        for chip in range(chips - steps)
+        for core in range(CORES)
+        for head in range(heads)
+    ]
+    return lax.ppermute(value, ("ctx", "head"), pairs)
+
+
+def pack_kernel(first_of, k_ref, v_ref, out_ref):
+    targets = out_ref.shape[0]
+    first = lax.axis_index("head") if first_of == "self" else 0
     for kind, ref in enumerate((k_ref, v_ref)):
-        for column in range(out_ref.shape[0] * GROUPS):
-            part = ref[:, column * HD : (column + 1) * HD]
-            out_ref[column // GROUPS, kind, column % GROUPS] = part
-
-
-def pack(keys, values, targets):
+        for slot in range(targets):
+            target = lax.rem(first + slot, targets)
+            for group in range(GROUPS):
+                column = (target * GROUPS + group) * HD
+                if first_of == "self":
+                    column = pl.multiple_of(column, HD)
+                out_ref[slot, kind, group] = ref[:, pl.ds(column, HD)]
+
+
+def pack(keys, values, targets, first_of):
     rows = keys.shape[0]
     return pl.pallas_call(
-        pack_kernel,
+        functools.partial(pack_kernel, first_of),
         out_shape=jax.ShapeDtypeStruct((targets, 2, GROUPS, rows, HD), keys.dtype),
-        name="pack",
+        name="pack_" + first_of,
     )(keys, values)
 
 
 def chunk(kv_ref, kind, group, first, count):
-    blocks, part = kv_ref.shape[0], kv_ref.shape[3]
-    return kv_ref[:, kind, group].reshape(blocks * part, HD)[first : first + count]
+    if kv_ref.ndim == 5:
+        rows = kv_ref[:, kind, group].reshape(-1, HD)
+    else:
+        heads = kv_ref.shape[0]
+        here = lax.axis_index("head")
+        turns = [lax.rem(here - source + heads, heads) for source in range(heads)]
+        rows = jnp.concatenate(
+            [kv_ref[turn, core, kind, group] for core in range(CORES) for turn in turns]
+        )
+    return rows[first : first + count]
 
 
 def with_ones(values):
@@ -236,7 +262,8 @@
 
 def near_part(queries, kv, starts, *state):
     shapes = [jax.ShapeDtypeStruct(part.shape, part.dtype) for part in state]
-    return call(near_kernel, "near", shapes, kv.shape[0] * kv.shape[3], queries, kv, starts, *state)
+    keys = CORES * queries.shape[0]
+    return call(near_kernel, "near", shapes, keys, queries, kv, starts, *state)
 
 
 def far_part(queries, kv, starts, *state):
@@ -244,20 +271,21 @@
     return call(far_kernel, "far", out, queries.shape[0], queries, kv, starts, *state)
 
 
-def attention(queries, own_both, first_both, second_both, doc_lengths):
-    starts, *state = own_part(queries, own_both, doc_lengths)
-    state = near_part(queries, first_both, starts, *state)
-    return far_part(queries, second_both, starts, *state)
-
-
 def local(queries, keys, values, doc_lengths):
-    targets = lax.axis_size("head")
-    packed = pack(keys, values, targets)
+    heads = lax.axis_size("head")
+    share = heads // CORES
+    core = lax.rem(lax.axis_index("ctx"), CORES)
+    turned = both_cores(pack(keys, values, heads, "self")[None])
+    pieces = [
+        lax.dynamic_index_in_dim(turned, core * share + j, axis=1, keepdims=False)
+        for j in range(share)
+    ]
+    first = [moved(piece, 1, lambda core, j=j: core * share + j) for j, piece in enumerate(pieces)]
+    packed = pack(keys, values, heads, "zero")
     own = lax.all_to_all(packed, "head", split_axis=0, concat_axis=0, tiled=True)
-    first = shifted(own, CORES)
+    first = jnp.stack(first)
+    second = shifted(first, CORES)
     starts, *state = own_part(queries, both_cores(own), doc_lengths)
-    first, starts = lax.optimization_barrier((first, starts))
-    second = shifted(first, CORES)
     state = near_part(queries, both_cores(first), starts, *state)
     return far_part(queries, both_cores(second), starts, *state)
 

time: 47.4 us -> 46 us (0.970)
  the two profiles are of different devices: /device:TPU:320 before, /device:TPU:249 now
where the time goes in v3:
time: 46 us; the launch traced here: 45.5 us
  starting transfers between devices  20.9 us (45%)
  Pallas kernels  13.1 us (28%)
  blocking collectives  11.3 us (25%)
    all_gather x4, blocking collectives, both_cores(): lax.all_gather(value, 'ctx', axis=0, tiled=True, axis_index_groups=pairs)  11.3 us
    ppermute x2, starting transfers between devices, moved(): return lax.ppermute(value, ('ctx', 'head'), pairs)  10.7 us
    pallas_call x3, Pallas kernels, call(): pl.pallas_call(kernel, out_shape=out_shape, compiler_params=pltpu.Compile...  9.35 us
    ppermute x1, starting transfers between devices, shifted(): lax.ppermute(value, 'ctx', [(at, at + steps) for at in range(count - step...  6.81 us
    pallas_call x2, Pallas kernels, pack(): pl.pallas_call(functools.partial(pack_kernel, first_of), out_shape=jax.Sh...  3.71 us
    all_to_all x1, starting transfers between devices, local(): lax.all_to_all(packed, 'head', split_axis=0, concat_axis=0, tiled=True)  3.46 us
  transfers between devices with their start and end apart: 4, of which 1 were waited for; matrix products, arithmetic and copies ran while one was open for 0% of the time, Pallas kernels for 21%

profile of v3, /device:TPU:249, one launch (start us, length us, event | category | flops | bytes accessed | tf_op | source)
XLA Modules:
  0.0 45.5 jit_solution(16861285265606398324)
XLA Ops:
  0.0 1.9 %pack_self.1 = bf16[4,2,2,96,128]{4,3,2,1,0:T(8,128)(2,1)} custom-call(bf16[96,1024]{1,0:T(8,128)(2,1)} %k_ref.3, bf16[96,1024]{1,0:T(8,128)(2,1)} %v_ref.3), custom_call_target="tpu_custom_call" | custom-call | tf_op jit(solution)/shard_map/pack_self/pallas_call | solution.py:61
  1.9 2.9 %all-gather = bf16[8,2,2,96,128]{4,3,2,1,0:T(8,128)(2,1)S(1)} all-gather(bf16[4,2,2,96,128]{4,3,2,1,0:T(8,128)(2,1)} %pack_self.1), channel_id=2, replica_groups={{0,4},{8,12},{16,20},{24,28},{32,36},{40,44},{48,52},{56,60},{64,68},{7..., dimensions={0}, use_global_device_ids=true | all-gather | bytes 1179648 | tf_op jit(solution)/shard_map/all_gather | solution.py:31
  4.8 6.9 %collective-permute-start = (bf16[2,2,2,96,128]{4,3,2,1,0:T(8,128)(2,1)S(1)}, bf16[2,2,2,96,128]{4,3,2,1,0:T(8,128)(2,1)S(1)}, u32[]{:S(2)}, u32[]{:S(2)}) collective-permute-start(bf16[2,2,2,96,128]{4,3,2,1,0:T(8,128)(2,1)S(1)} %get-tuple-element.19), channel_id=1, source_target_pairs={{0,8},{1,9},{2,10},{3,11},{4,14},{5,15},{6,12},{7,13},{8,16},{9,17... | collective-permute-start | bytes 589832 | tf_op jit(solution)/shard_map/ppermute | solution.py:43
  11.7 3.8 %collective-permute-start.1 = (bf16[2,2,2,96,128]{4,3,2,1,0:T(8,128)(2,1)S(1)}, bf16[2,2,2,96,128]{4,3,2,1,0:T(8,128)(2,1)S(1)}, u32[]{:S(2)}, u32[]{:S(2)}) collective-permute-start(bf16[2,2,2,96,128]{4,3,2,1,0:T(8,128)(2,1)S(1)} %get-tuple-element.20), channel_id=1, source_target_pairs={{0,9},{1,10},{2,11},{3,8},{4,15},{5,12},{6,13},{7,14},{8,17},{9,18... | collective-permute-start | bytes 589832 | tf_op jit(solution)/shard_map/ppermute | solution.py:43
  15.4 1.8 %pack_zero.1 = bf16[4,2,2,96,128]{4,3,2,1,0:T(8,128)(2,1)} custom-call(bf16[96,1024]{1,0:T(8,128)(2,1)} %k_ref.3, bf16[96,1024]{1,0:T(8,128)(2,1)} %v_ref.3), custom_call_target="tpu_custom_call" | custom-call | tf_op jit(solution)/shard_map/pack_zero/pallas_call | solution.py:61
  17.3 3.5 %all-to-all-start = ((bf16[4,2,2,96,128]{4,3,2,1,0:T(8,128)(2,1)}), bf16[4,2,2,96,128]{4,3,2,1,0:T(8,128)(2,1)S(1)}, u32[]{:S(2)}, u32[]{:S(2)}) async-start(bf16[4,2,2,96,128]{4,3,2,1,0:T(8,128)(2,1)} %pack_zero.1), calls=%async_computation | async-start | bytes 786432 | tf_op jit(solution)/shard_map/all_to_all | solution.py:285
  20.7 0.0 collective-permute-done
  20.8 0.1 collective-permute-done.1
  20.8 0.0 copy-start
  20.8 0.0 copy-start.1
  20.9 6.8 %collective-permute-start.2 = (bf16[2,2,2,2,96,128]{5,4,3,2,1,0:T(8,128)(2,1)S(1)}, bf16[2,2,2,2,96,128]{5,4,3,2,1,0:T(8,128)(2,1)S(1)}, u32[]{:S(2)}, u32[]{:S(2)}) collective-permute-start(bf16[2,2,2,2,96,128]{5,4,3,2,1,0:T(8,128)(2,1)S(1)} %pad_maximum_fusion), channel_id=1, source_target_pairs={{0,8},{4,12},{8,16},{12,20},{16,24},{20,28},{24,32},{28,36},{32,40... | collective-permute-start | bytes 1179656 | tf_op jit(solution)/shard_map/ppermute | solution.py:25
  27.7 3.7 %all_gather.15.kv_ref = bf16[4,2,2,2,96,128]{5,4,3,2,1,0:T(8,128)(2,1)S(1)} all-gather(bf16[2,2,2,2,96,128]{5,4,3,2,1,0:T(8,128)(2,1)S(1)} %pad_maximum_fusion), channel_id=1, replica_groups={{0,4},{8,12},{16,20},{24,28},{32,36},{40,44},{48,52},{56,60},{64,68},{7..., dimensions={0}, use_global_device_ids=true | all-gather | bytes 1179648 | tf_op jit(solution)/shard_map/all_gather | solution.py:31
  31.4 0.0 all-to-all-done
  31.4 2.4 %all_gather.14.kv_ref = bf16[8,2,2,96,128]{4,3,2,1,0:T(8,128)(2,1)S(1)} all-gather(bf16[4,2,2,96,128]{4,3,2,1,0:T(8,128)(2,1)S(1)} %all-to-all-done), channel_id=1, replica_groups={{0,4},{8,12},{16,20},{24,28},{32,36},{40,44},{48,52},{56,60},{64,68},{7..., dimensions={0}, use_global_device_ids=true | all-gather | bytes 1179648 | tf_op jit(solution)/shard_map/all_gather | solution.py:31
  33.8 0.0 copy-done
  33.8 0.0 copy-done.1
  33.8 3.4 %own.1 = (f32[384,128]{1,0:T(8,128)S(1)}, f32[8,384,128]{2,1,0:T(8,128)S(1)}, f32[8,384,128]{2,1,0:T(8,128)S(1)}, f32[8,384,128]{2,1,0:T(8,128)S(1)}) custom-call(bf16[384,1024]{1,0:T(8,128)(2,1)S(1)} %copy-done, bf16[8,2,2,96,128]{4,3,2,1,0:T(8,128)(2,1)S(1)} %all_gather.14.kv_ref, s32[1,512]{1,0:T(1,128)S(1)} %bitcast.8), custom_call_target="tpu_custom_call" | custom-call | flops 1811939328 | bytes 3145728 | tf_op jit(solution)/shard_map/own/pallas_call | solution.py:245
  37.2 4.5 %near.1 = (f32[8,384,128]{2,1,0:T(8,128)S(1)}, f32[8,384,128]{2,1,0:T(8,128)S(1)}, f32[8,384,128]{2,1,0:T(8,128)S(1)}) custom-call(bf16[384,1024]{1,0:T(8,128)(2,1)S(1)} %copy-done, bf16[4,2,2,2,96,128]{5,4,3,2,1,0:T(8,128)(2,1)S(1)} %all_gather.15.kv_ref, f32[384,128]{1,0:T(8,128)S(1)} %get-tuple-element.12.starts_ref, ...), custom_call_target="tpu_custom_call" | custom-call | flops 1811939328 | bytes 3145728 | tf_op jit(solution)/shard_map/near/pallas_call | solution.py:245
  41.7 0.0 collective-permute-done.2
  41.7 2.4 %all_gather.13.kv_ref = bf16[4,2,2,2,96,128]{5,4,3,2,1,0:T(8,128)(2,1)S(1)} all-gather(bf16[2,2,2,2,96,128]{5,4,3,2,1,0:T(8,128)(2,1)S(1)} %collective-permute-done.2), channel_id=1, replica_groups={{0,4},{8,12},{16,20},{24,28},{32,36},{40,44},{48,52},{56,60},{64,68},{7..., dimensions={0}, use_global_device_ids=true | all-gather | bytes 1179648 | tf_op jit(solution)/shard_map/all_gather | solution.py:31
  44.1 1.4 %far.1 = bf16[384,1024]{1,0:T(8,128)(2,1)} custom-call(bf16[384,1024]{1,0:T(8,128)(2,1)S(1)} %copy-done, bf16[4,2,2,2,96,128]{5,4,3,2,1,0:T(8,128)(2,1)S(1)} %all_gather.13.kv_ref, f32[384,128]{1,0:T(8,128)S(1)} %get-tuple-element.12.starts_ref, f32[8,384,128]{2,1,0:T(8,128)S(1)} %get-tuple-element.16.acc_in, f32[8,384,128]{2,1,0:T(8,128)S(1)} %get-tuple-element.17.sum_in, ...), custom_call_target="tpu_custom_call" | custom-call | flops 905969664 | bytes 3145728 | tf_op jit(solution)/shard_map/far/pallas_call | solution.py:245
  (2 shorter events, 0.1 us)
Async XLA Ops:
  4.8 16.0 %collective-permute-start = (bf16[2,2,2,96,128]{4,3,2,1,0:T(8,128)(2,1)S(1)}, bf16[2,2,2,96,128]{4,3,2,1,0:T(8,128)(2,1)S(1)}, u32[]{:S(2)}, u32[]{:S(2)}) collective-permute-start(bf16[2,2,2,96,128]{4,3,2,1,0:T(8,128)(2,1)S(1)} %get-tuple-element.19), channel_id=1, source_target_pairs={{0,8},{1,9},{2,10},{3,11},{4,14},{5,15},{6,12},{7,13},{8,16},{9,17... | collective-permute-start | bytes 589832 | tf_op jit(solution)/shard_map/ppermute | solution.py:43
  11.7 9.2 %collective-permute-start.1 = (bf16[2,2,2,96,128]{4,3,2,1,0:T(8,128)(2,1)S(1)}, bf16[2,2,2,96,128]{4,3,2,1,0:T(8,128)(2,1)S(1)}, u32[]{:S(2)}, u32[]{:S(2)}) collective-permute-start(bf16[2,2,2,96,128]{4,3,2,1,0:T(8,128)(2,1)S(1)} %get-tuple-element.20), channel_id=1, source_target_pairs={{0,9},{1,10},{2,11},{3,8},{4,15},{5,12},{6,13},{7,14},{8,17},{9,18... | collective-permute-start | bytes 589832 | tf_op jit(solution)/shard_map/ppermute | solution.py:43
  17.3 14.1 %all-to-all-start = ((bf16[4,2,2,96,128]{4,3,2,1,0:T(8,128)(2,1)}), bf16[4,2,2,96,128]{4,3,2,1,0:T(8,128)(2,1)S(1)}, u32[]{:S(2)}, u32[]{:S(2)}) async-start(bf16[4,2,2,96,128]{4,3,2,1,0:T(8,128)(2,1)} %pack_zero.1), calls=%async_computation | async-start | bytes 786432 | tf_op jit(solution)/shard_map/all_to_all | solution.py:285
  20.8 12.9 %copy-start = (bf16[384,1024]{1,0:T(8,128)(2,1)S(1)}, bf16[384,1024]{1,0:T(8,128)(2,1)}, u32[]{:S(2)}) copy-start(bf16[384,1024]{1,0:T(8,128)(2,1)} %q_ref.5) | copy-start | bytes 2359300
  20.8 12.9 %copy-start.1 = (s32[512]{0:T(512)S(1)}, s32[512]{0:T(512)}, u32[]{:S(2)}) copy-start(s32[512]{0:T(512)} %param.7) | copy-start | bytes 6148
  20.9 20.8 %collective-permute-start.2 = (bf16[2,2,2,2,96,128]{5,4,3,2,1,0:T(8,128)(2,1)S(1)}, bf16[2,2,2,2,96,128]{5,4,3,2,1,0:T(8,128)(2,1)S(1)}, u32[]{:S(2)}, u32[]{:S(2)}) collective-permute-start(bf16[2,2,2,2,96,128]{5,4,3,2,1,0:T(8,128)(2,1)S(1)} %pad_maximum_fusion), channel_id=1, source_target_pairs={{0,8},{4,12},{8,16},{12,20},{16,24},{20,28},{24,32},{28,36},{32,40... | collective-permute-start | bytes 1179656 | tf_op jit(solution)/shard_map/ppermute | solution.py:25
